TPU v7x, 256 devices: a whole 4x4x8 slice. The times are simulated.
256 devices in a mesh: ctx: 32 (over z, y), tp: 8 (over x, core).
Axes of the slice: x: 4, y: 4, z: 8, core: 2. Of those that a mesh axis runs over, the one named last changes fastest.
Arguments:
- q_nope: bfloat16 [1, 4096, 8192], P(None, 'ctx', 'tp'), may hold values from -6 to 6
- q_rope: bfloat16 [1, 4096, 4096], P(None, 'ctx', 'tp'), may hold values from -8 to 8
- latent_keys: bfloat16 [1, 4096, 576], P(None, 'ctx'), may hold values from -8 to 8
- group_order: int32 [64], replicated, may hold values from 0 to 63, as said below
- w_uk: bfloat16 [64, 128, 512], P('tp'), may hold values from -0.5 to 0.5
- w_uv: bfloat16 [64, 512, 128], P('tp'), may hold values from -0.25 to 0.25
- o_proj: bfloat16 [8192, 3584], P('tp'), may hold values from -0.0625 to 0.0625
Outputs:
- mixed: bfloat16 [1, 4096, 3584], P(None, 'ctx')
Inputs may be any that keep to these rules, and one draw needn't show every extreme that they name: `group_order`: a permutation of the group numbers in which slots 2j and 2j + 1 hold two groups whose numbers add up to 63.
All inputs are finite; a program needn't handle non-finite values.
Results may differ from a plain program's by a relative error of at most 0.02.
Values may be sent and summed in bfloat16 or wider, within the bound.
A program may use at most 128 MiB of HBM per device.

v0:
```python
import functools
import math

import jax
import jax.numpy as jnp
import numpy as np
from jax import lax
from jax.experimental import pallas as pl
from jax.experimental.pallas import tpu as pltpu
from jax.sharding import PartitionSpec as P

MESH = pl.DeviceIdType.MESH
NY, NZ, NX = 4, 8, 4
HEADS, NOPE, ROPE, LATENT, VDIM, OUT = 8, 128, 64, 512, 128, 3584
GROUP = 64
TOK = 2 * GROUP
HALF = LATENT // 2
COLS = OUT // 2
SHARDS = NY * NZ
BATCH = 4
BATCHES = SHARDS // BATCH
ROWS = TOK * HEADS
MSG = TOK + 16
KW = LATENT + 128
PIECES = 2
PIECE = COLS // PIECES
LAST = BATCH * (BATCHES - 1)
HIDDEN = -1e30
SCORE_SCALE = (NOPE + ROPE) ** -0.5 * math.log2(math.e)

TREE = {
    (0, 1): (0, 0),
    (2, 0): (0, 0),
    (1, 0): (0, 0),
    (3, 0): (0, 0),
    (0, 2): (0, 0),
    (0, -3): (0, 0),
    (1, 1): (0, 1),
    (3, 1): (0, 1),
    (2, 1): (2, 0),
    (0, -2): (0, 0),
    (2, -1): (2, 0),
    (0, 3): (0, 2),
    (3, 2): (0, 2),
    (0, -1): (0, 0),
    (1, -1): (1, 0),
    (0, 4): (0, -3),
    (1, 2): (1, 1),
    (1, -2): (0, -2),
    (1, -3): (0, -3),
    (3, -3): (0, -3),
    (2, -2): (2, -1),
    (2, 2): (2, 1),
    (3, -1): (2, -1),
    (3, -2): (0, -2),
    (3, 3): (0, 3),
    (1, 4): (0, 4),
    (1, 3): (0, 3),
    (3, 4): (0, 4),
    (2, 3): (2, 1),
    (2, 4): (2, -1),
    (2, -3): (1, -3),
}
SIDES = {
    (0, -3): 3,
    (0, -2): 1,
    (0, -1): 3,
    (0, 4): 3,
    (1, -2): 1,
    (1, -3): 3,
    (3, -3): 3,
    (3, -2): 3,
    (1, 4): 3,
    (3, 4): 1,
    (2, -3): 1,
}
OFFSETS = (
    (0, 0),
    (0, 1),
    (2, 0),
    (1, 0),
    (3, 0),
    (0, 2),
    (0, -3),
    (1, 1),
    (3, 1),
    (2, 1),
    (0, -2),
    (2, -1),
    (0, 3),
    (3, 2),
    (0, -1),
    (1, -1),
    (0, 4),
    (1, 2),
    (1, -2),
    (1, -3),
    (3, -3),
    (2, -2),
    (2, 2),
    (3, -1),
    (3, -2),
    (3, 3),
    (1, 4),
    (1, 3),
    (3, 4),
    (2, 3),
    (2, 4),
    (2, -3),
)
SENDS = (
    ("half", (0, -3)),
    ("full", (2, 0)),
    ("full", (0, 1)),
    ("full", (0, 2)),
    ("half", (0, -2)),
    ("full", (1, 0)),
    ("half", (0, -1)),
    ("full", (3, 0)),
    ("full", (1, 1)),
    ("full", (3, 1)),
    ("half", (1, -3)),
    ("half", (0, 4)),
    ("side", (0, -3)),
    ("half", (3, -3)),
    ("full", (2, -1)),
    ("full", (2, 1)),
    ("full", (1, -1)),
    ("side", (0, -2)),
    ("half", (1, -2)),
    ("half", (3, -2)),
    ("full", (0, 3)),
    ("full", (3, 2)),
    ("side", (0, -1)),
    ("full", (1, 2)),
    ("side", (0, 4)),
    ("half", (1, 4)),
    ("half", (3, 4)),
    ("side", (1, -3)),
    ("half", (2, -3)),
    ("side", (3, -3)),
    ("full", (2, 2)),
    ("full", (2, 3)),
    ("side", (1, -2)),
    ("side", (3, -2)),
    ("full", (2, -2)),
    ("full", (3, -1)),
    ("full", (2, 4)),
    ("full", (1, 3)),
    ("full", (3, 3)),
    ("side", (1, 4)),
    ("side", (3, 4)),
    ("side", (2, -3)),
)
PLAN = (
    ("full", (0, 1)),
    ("half", (0, -3)),
    ("full", (2, 0)),
    ("full", (1, 0)),
    ("full", (3, 0)),
    ("half", (0, -2)),
    ("full", (0, 2)),
    ("attend", 0),
    ("half", (0, -1)),
    ("side", (0, -3)),
    ("full", (1, 1)),
    ("full", (3, 1)),
    ("half", (0, 4)),
    ("half", (1, -3)),
    ("half", (3, -3)),
    ("full", (2, 1)),
    ("side", (0, -2)),
    ("half", (1, -2)),
    ("half", (3, -2)),
    ("full", (2, -1)),
    ("attend", 1),
    ("full", (0, 3)),
    ("full", (3, 2)),
    ("side", (0, -1)),
    ("full", (1, -1)),
    ("attend", 2),
    ("half", (1, 4)),
    ("half", (3, 4)),
    ("side", (0, 4)),
    ("full", (1, 2)),
    ("half", (2, -3)),
    ("side", (1, -2)),
    ("side", (1, -3)),
    ("attend", 3),
    ("side", (3, -3)),
    ("full", (2, -2)),
    ("full", (2, 2)),
    ("full", (3, -1)),
    ("side", (3, -2)),
    ("attend", 4),
    ("full", (3, 3)),
    ("side", (1, 4)),
    ("full", (1, 3)),
    ("side", (3, 4)),
    ("attend", 5),
    ("full", (2, 3)),
    ("full", (2, 4)),
    ("side", (2, -3)),
    ("attend", 6),
    ("attend", 7, (("heads", 0),)),
    ("heads", 1),
    ("exchange", 0),
    ("exchange", 1),
    ("keep", 0),
    ("scatter", 0, 0),
    ("scatter", 1, 0),
    ("keep", 1),
    ("scatter", 0, 1),
    ("scatter", 1, 1),
    ("settle",),
    ("share", 0, 0),
    ("share", 1, 0),
    ("share", 0, 1),
    ("share", 1, 1),
    ("forward", 0, 0),
    ("forward", 1, 0),
    ("forward", 0, 1),
    ("forward", 1, 1),
)
SLOT = {offset: at for at, offset in enumerate(OFFSETS)}


def step_of(offset, parent):
    return ((offset[0] - parent[0]) % NY, (offset[1] - parent[1]) % NZ)


STEPS = sorted({step_of(o, p) for o, p in TREE.items()} | {step_of(p, o) for o, p in TREE.items()})


def dot_nt(a, b):
    return lax.dot_general(a, b, (((1,), (1,)), ((), ())), preferred_element_type=jnp.float32)


def attention_kernel(
    order,
    qn_hbm,
    qr_hbm,
    lk_hbm,
    wuk_hbm,
    wuv_hbm,
    op_hbm,
    out,
    qn,
    qr,
    lk,
    wuk,
    wuv,
    op,
    kr,
    kbuf,
    qa,
    qb,
    klo,
    khi,
    bias,
    top,
    total,
    acc,
    flat,
    xsend,
    xrecv,
    own,
    part,
    rsr,
    obuf,
    load_sem,
    ring_send,
    ring_recv,
    pair_send,
    pair_recv,
    ex_send,
    ex_recv,
    rs_send,
    rs_recv,
    ag_send,
    ag_recv,
    fw_send,
    fw_recv,
):
    ctx = lax.axis_index("ctx")
    tp = lax.axis_index("tp")
    z, y = ctx // NY, lax.rem(ctx, NY)
    x, c = tp // 2, lax.rem(tp, 2)

    def ring_peer(step):
        dy, dz = step
        return (lax.rem(z + dz, NZ) * NY + lax.rem(y + dy, NY), tp)

    def x_peer(d):
        return (ctx, lax.rem(x + d, NX) * 2 + c)

    partner = (ctx, x * 2 + 1 - c)
    peers = [ring_peer(s) for s in STEPS] + [x_peer(d) for d in (1, 2, 3)] + [partner]
    barrier = pltpu.get_barrier_semaphore()
    for peer in peers:
        pl.semaphore_signal(barrier, inc=1, device_id=peer, device_id_type=MESH)

    loads = [
        pltpu.make_async_copy(src, dst, load_sem.at[at])
        for at, (src, dst) in enumerate(
            [(lk_hbm, lk), (qn_hbm, qn), (qr_hbm, qr), (wuk_hbm, wuk), (wuv_hbm, wuv), (op_hbm, op)]
        )
    ]
    for load in loads:
        load.start()

    g0 = order[2 * ctx]
    g1 = order[2 * ctx + 1]
    swap = g0 > g1
    low = jnp.minimum(g0, g1)

    def sort_rows(value):
        first, second = value[:GROUP], value[GROUP:]
        return jnp.where(swap, second, first), jnp.where(swap, first, second)

    lane = lax.broadcasted_iota(jnp.int32, (TOK, 128), 1)
    row = lax.broadcasted_iota(jnp.int32, (TOK, 128), 0)
    position = jnp.where(row < GROUP, low * GROUP + row, (63 - low) * GROUP + row - GROUP)
    frequencies = np.float32(10000.0) ** (-np.arange(32, dtype=np.float32) / np.float32(32))
    freq_lane = lax.rem(lax.broadcasted_iota(jnp.int32, (8, 128), 1), 32)
    freq = jnp.zeros((8, 128), jnp.float32)
    for at in range(32):
        freq = jnp.where(freq_lane == at, float(frequencies[at]), freq)
    angle = position.astype(jnp.float32) * freq[:1]
    cosine, sine = jnp.cos(angle), jnp.sin(angle)
    first_half = lax.rem(lane, ROPE) < ROPE // 2

    def rotate(value):
        other = jnp.where(first_half, -pltpu.roll(value, 96, 1), pltpu.roll(value, 32, 1))
        return value * cosine + other * sine

    loads[0].wait()
    keys = jnp.transpose(lk[...].astype(jnp.float32))
    lat_lo, lat_hi = sort_rows(keys[:, :LATENT].astype(jnp.bfloat16))
    for half in range(2):
        kbuf[half, 0, 0:GROUP, :] = lat_lo[:, half * HALF : (half + 1) * HALF]
        kbuf[half, 0, GROUP + 16 : MSG, :] = lat_hi[:, half * HALF : (half + 1) * HALF]
    kr[...] = jnp.zeros_like(kr)
    kr[:, :ROPE] = keys[:, LATENT:]
    rope_rows = kr[...]
    rope_rows = rope_rows + pltpu.roll(rope_rows, ROPE, 1)
    rotated = rotate(jnp.concatenate(sort_rows(rope_rows), 0))
    packed = jnp.where(lane[:GROUP] < ROPE, rotated[:GROUP], rotated[GROUP:]).astype(jnp.bfloat16)
    for at in range(4):
        kbuf[at // 2, 0, GROUP : GROUP + 16, (at % 2) * 128 : (at % 2 + 1) * 128] = packed[
            at * 16 : (at + 1) * 16
        ]

    pl.semaphore_wait(barrier, len(peers))

    def ring_block(offset, kind, other=False):
        if kind == "full":
            return kbuf.at[c, SLOT[offset]]
        parity = lax.rem(x, 2)
        first = (1 - parity if other else parity) * (HALF // 2)
        return kbuf.at[c, SLOT[offset], :, pl.ds(pl.multiple_of(first, 128), HALF // 2)]

    def ring_copy(kind, offset, arriving=False):
        side = kind == "side"
        sem = (SHARDS if side else 0) + SLOT[offset]
        return pltpu.make_async_remote_copy(
            src_ref=ring_block(offset if side else TREE[offset], kind, arriving and side),
            dst_ref=ring_block(offset, kind, arriving and side),
            send_sem=ring_send.at[sem],
            recv_sem=ring_recv.at[sem],
            device_id=x_peer(SIDES[offset]) if side else ring_peer(step_of(offset, TREE[offset])),
            device_id_type=MESH,
        )

    ring = {send: ring_copy(*send) for send in SENDS}

    def hand_on(kind, offset):
        for send in SENDS:
            if send[0] == "side":
                if kind == "half" and send[1] == offset:
                    ring[send].start()
            elif kind != "side" and TREE[send[1]] == offset:
                ring[send].start()

    hand_on("full", (0, 0))

    def pair_copy(first, count):
        rows = kbuf.at[c, pl.ds(first, count)]
        return pltpu.make_async_remote_copy(
            src_ref=rows,
            dst_ref=rows,
            send_sem=pair_send.at[first],
            recv_sem=pair_recv.at[first],
            device_id=partner,
            device_id_type=MESH,
        )

    spans = [(max(1, at), min(at + BATCH, SHARDS) - max(1, at)) for at in range(0, LAST, BATCH)]
    spans += [(at, 1) for at in range(LAST, SHARDS)]
    pairs = {first + count - 1: pair_copy(first, count) for first, count in spans}

    key_lane = lax.broadcasted_iota(jnp.int32, (1, BATCH * GROUP), 1)

    def mask_row(offsets, visible):
        line = jnp.zeros((1, BATCH * GROUP), jnp.float32)
        for at, (dy, dz) in enumerate(offsets):
            if (dy, dz) != (0, 0):
                owner = lax.rem(z - dz + NZ, NZ) * NY + lax.rem(y - dy + NY, NY)
                key_low = jnp.minimum(order[2 * owner], order[2 * owner + 1])
                here = key_lane // GROUP == at
                line = jnp.where(here, jnp.where(visible(key_low), 0.0, HIDDEN), line)
        return line

    for batch in range(BATCHES):
        span = slice(batch * BATCH, (batch + 1) * BATCH)
        bias[batch, 0:1, :] = mask_row(OFFSETS[span], lambda key_low: key_low < low)
        bias[batch, 8:9, :] = mask_row(OFFSETS[span], lambda key_low: key_low > low)

    top[...] = jnp.full_like(top, HIDDEN)
    total[...] = jnp.zeros_like(total)

    @pl.loop(0, ROWS // GROUP)
    def _(at):
        acc[pl.ds(at * GROUP, GROUP), :] = jnp.zeros((GROUP, LATENT), jnp.float32)

    loads[2].wait()
    for block in range(HEADS // 2):
        rows = qr[:, block * 128 : (block + 1) * 128].astype(jnp.float32)
        rotated = rotate(jnp.concatenate(sort_rows(rows), 0)) * SCORE_SCALE
        shifted = pltpu.roll(rotated, ROPE, 1)
        for odd in range(2):
            head = 2 * block + odd
            for_low = jnp.where(lane < ROPE, shifted if odd else rotated, 0.0).astype(jnp.bfloat16)
            for_high = jnp.where(lane < ROPE, 0.0, rotated if odd else shifted).astype(jnp.bfloat16)
            at = head * GROUP
            qa[at : at + GROUP, LATENT:] = for_low[:GROUP]
            qa[ROWS // 2 + at : ROWS // 2 + at + GROUP, LATENT:] = for_low[GROUP:]
            qb[at : at + GROUP, LATENT:] = for_high[GROUP:]
    loads[1].wait()
    loads[3].wait()
    for head in range(HEADS):
        rows = jnp.concatenate(sort_rows(qn[:, head * NOPE : (head + 1) * NOPE]), 0)
        absorbed = jnp.dot(rows, wuk[head], preferred_element_type=jnp.float32) * SCORE_SCALE
        absorbed = absorbed.astype(jnp.bfloat16)
        at = head * GROUP
        qa[at : at + GROUP, :LATENT] = absorbed[:GROUP]
        qa[ROWS // 2 + at : ROWS // 2 + at + GROUP, :LATENT] = absorbed[GROUP:]
        qb[at : at + GROUP, :LATENT] = absorbed[GROUP:]

    def update(rows, scores, values):
        pieces = [s[:, at : at + 128] for s in scores for at in range(0, s.shape[1], 128)]
        peak = functools.reduce(jnp.maximum, pieces)
        before = top[rows, :]
        now = jnp.maximum(before, jnp.max(peak, 1, keepdims=True))
        fade = jnp.exp2(before - now)
        weights = [jnp.exp2(piece - now) for piece in pieces]
        top[rows, :] = now
        total[rows, :] = total[rows, :] * fade + functools.reduce(jnp.add, weights)
        summed = None
        per = len(weights) // len(values)
        for at, value in enumerate(values):
            mine = jnp.concatenate(
                [w.astype(jnp.bfloat16) for w in weights[at * per : (at + 1) * per]], 1
            )
            part_sum = jnp.dot(mine, value[:, :LATENT], preferred_element_type=jnp.float32)
            summed = part_sum if summed is None else summed + part_sum
        for at in range(0, LATENT, 128):
            acc[rows, at : at + 128] = acc[rows, at : at + 128] * fade + summed[:, at : at + 128]

    def gather_keys(batch):
        for at in range(BATCH):
            slot = batch * BATCH + at
            rows = slice(at * GROUP, (at + 1) * GROUP)
            for half in range(2):
                cols = slice(half * HALF, (half + 1) * HALF)
                klo[rows, cols] = kbuf[half, slot, 0:GROUP, :]
                khi[rows, cols] = kbuf[half, slot, GROUP + 16 : MSG, :]
            for piece in range(4):
                rotary = kbuf[
                    piece // 2, slot, GROUP : GROUP + 16, (piece % 2) * 128 : (piece % 2 + 1) * 128
                ]
                at_row = at * GROUP + piece * 16
                klo[at_row : at_row + 16, LATENT:] = rotary
                khi[at_row : at_row + 16, LATENT:] = rotary

    def own_mask(scores):
        key = lax.broadcasted_iota(jnp.int32, scores.shape, 1)
        token = lax.rem(lax.broadcasted_iota(jnp.int32, scores.shape, 0), GROUP)
        return jnp.where((key < GROUP) & (key > token), HIDDEN, scores)

    low_rows, high_rows = pl.ds(0, ROWS // 2), pl.ds(ROWS // 2, ROWS // 2)

    def score(batch):
        for slot in range(batch * BATCH, (batch + 1) * BATCH):
            if slot in pairs:
                pairs[slot].wait_recv()
        gather_keys(batch)
        low_low = dot_nt(qa[low_rows, :], klo[...]) + bias[batch, 0:1, :]
        high_low = dot_nt(qa[high_rows, :], klo[...])
        high_high = dot_nt(qb[...], khi[...]) + bias[batch, 8:9, :]
        if batch == 0:
            low_low, high_high = own_mask(low_low), own_mask(high_high)
        return [low_low], [high_low, high_high]

    def attend(batch, between=()):
        low_scores, high_scores = score(batch)
        update(low_rows, low_scores, [klo])
        for step in between:
            run(step)
        update(high_rows, high_scores, [klo, khi])

    def column(core, piece):
        return pl.multiple_of(core * COLS + piece * PIECE, 128)

    def exchange_copy(group, piece):
        return pltpu.make_async_remote_copy(
            src_ref=xsend.at[group, piece],
            dst_ref=xrecv.at[group, piece],
            send_sem=ex_send.at[group, piece],
            recv_sem=ex_recv.at[group, piece],
            device_id=partner,
            device_id_type=MESH,
        )

    def scatter_copy(group, piece, d):
        to = lax.rem(x + d, NX)
        return pltpu.make_async_remote_copy(
            src_ref=part.at[group, piece, pl.ds(pl.multiple_of(to * 16, 16), 16)],
            dst_ref=rsr.at[group, piece, d - 1],
            send_sem=rs_send.at[group, piece, d - 1],
            recv_sem=rs_recv.at[group, piece, d - 1],
            device_id=x_peer(d),
            device_id_type=MESH,
        )

    def out_piece(group, piece, chip):
        rows = pl.ds(pl.multiple_of(group * GROUP + chip * 16, 16), 16)
        return obuf.at[rows, pl.ds(column(c, piece), PIECE)]

    def share_copy(group, piece, d):
        block = out_piece(group, piece, x)
        return pltpu.make_async_remote_copy(
            src_ref=block,
            dst_ref=block,
            send_sem=ag_send.at[group, piece, d],
            recv_sem=ag_recv.at[group, piece, d],
            device_id=x_peer(d) if d else partner,
            device_id_type=MESH,
        )

    def forward_copy(group, piece, d):
        block = out_piece(group, piece, lax.rem(x + NX - d, NX))
        return pltpu.make_async_remote_copy(
            src_ref=block,
            dst_ref=block,
            send_sem=fw_send.at[group, piece, d - 1],
            recv_sem=fw_recv.at[group, piece, d - 1],
            device_id=partner,
            device_id_type=MESH,
        )

    def heads(group):
        if group == 0:
            loads[4].wait()
            loads[5].wait()
        for head in range(HEADS):
            rows = pl.ds(group * (ROWS // 2) + head * GROUP, GROUP)
            norm = 1.0 / jnp.sum(total[rows, :], 1, keepdims=True)
            context = (acc[rows, :] * norm).astype(jnp.bfloat16)
            flat[group * GROUP : (group + 1) * GROUP, head * VDIM : (head + 1) * VDIM] = jnp.dot(
                context, wuv[head], preferred_element_type=jnp.float32
            ).astype(jnp.bfloat16)

    def partial_out(core, piece):
        return jnp.dot(
            flat[...], op[:, pl.ds(column(core, piece), PIECE)], preferred_element_type=jnp.float32
        )

    def exchange(piece):
        sums = partial_out(1 - c, piece).astype(jnp.bfloat16)
        for group in range(2):
            xsend[group, piece] = sums[group * GROUP : (group + 1) * GROUP]
            exchange_copy(group, piece).start()

    def keep(piece):
        sums = partial_out(c, piece)
        for group in range(2):
            own[group, piece] = sums[group * GROUP : (group + 1) * GROUP]

    def scatter(group, piece):
        exchange_copy(group, piece).wait_recv()
        summed = own[group, piece] + xrecv[group, piece].astype(jnp.float32)
        own[group, piece] = summed
        part[group, piece] = summed.astype(jnp.bfloat16)
        for d in (2, 1, 3):
            scatter_copy(group, piece, d).start()

    def share(group, piece):
        for d in (1, 2, 3):
            scatter_copy(group, piece, d).wait_recv()
        summed = own[group, piece, pl.ds(pl.multiple_of(x * 16, 16), 16), :]
        for d in range(3):
            summed = summed + rsr[group, piece, d].astype(jnp.float32)
        rows = pl.ds(pl.multiple_of(group * GROUP + x * 16, 16), 16)
        obuf[rows, pl.ds(column(c, piece), PIECE)] = summed.astype(jnp.bfloat16)
        for d in (2, 1, 3, 0):
            share_copy(group, piece, d).start()

    def forward(group, piece):
        for d in (1, 3, 2):
            share_copy(group, piece, d).wait_recv()
            forward_copy(group, piece, d).start()

    def settle_gather():
        for send in SENDS:
            ring[send].wait_send()
        for pair in pairs.values():
            pair.wait_send()

    def arrive(kind, offset):
        (ring_copy(kind, offset, True) if kind == "side" else ring[kind, offset]).wait_recv()
        hand_on(kind, offset)
        if kind != "half" and SLOT[offset] in pairs:
            pairs[SLOT[offset]].start()

    steps = {
        "attend": attend,
        "heads": heads,
        "exchange": exchange,
        "keep": keep,
        "scatter": scatter,
        "share": share,
        "forward": forward,
        "settle": settle_gather,
    }

    def run(step):
        if step[0] in steps:
            steps[step[0]](*step[1:])
        else:
            arrive(*step)

    for step in PLAN:
        run(step)

    tail = [(group, piece) for group in range(2) for piece in range(PIECES)]
    for group, piece in tail:
        share_copy(group, piece, 0).wait_recv()
        for d in (1, 2, 3):
            forward_copy(group, piece, d).wait_recv()
    for at in range(0, OUT, PIECE):
        cols = slice(at, at + PIECE)
        first, second = sort_rows(obuf[:, cols])
        out[:GROUP, cols] = first
        out[GROUP:, cols] = second
    for group, piece in tail:
        exchange_copy(group, piece).wait_send()
        share_copy(group, piece, 0).wait_send()
        for d in (1, 2, 3):
            scatter_copy(group, piece, d).wait_send()
            share_copy(group, piece, d).wait_send()
            forward_copy(group, piece, d).wait_send()


def on_device(q_nope, q_rope, latent_keys, group_order, w_uk, w_uv, o_proj):
    bf16, f32 = jnp.bfloat16, jnp.float32
    anywhere = pl.BlockSpec(memory_space=pl.ANY)
    vmem, dma = pltpu.VMEM, pltpu.SemaphoreType.DMA
    rows = pl.pallas_call(
        attention_kernel,
        out_shape=pltpu.VMEM((TOK, OUT), bf16),
        in_specs=[pl.BlockSpec(memory_space=pltpu.SMEM)] + [anywhere] * 6,
        out_specs=pl.BlockSpec(memory_space=pltpu.VMEM),
        scratch_shapes=[
            vmem((TOK, HEADS * NOPE), bf16),
            vmem((TOK, HEADS * ROPE), bf16),
            vmem((LATENT + ROPE, TOK), bf16),
            vmem((HEADS, NOPE, LATENT), bf16),
            vmem((HEADS, LATENT, VDIM), bf16),
            vmem((HEADS * VDIM, OUT), bf16),
            vmem((TOK, 128), f32),
            vmem((2, SHARDS, MSG, HALF), bf16),
            vmem((ROWS, KW), bf16),
            vmem((ROWS // 2, KW), bf16),
            vmem((BATCH * GROUP, KW), bf16),
            vmem((BATCH * GROUP, KW), bf16),
            vmem((BATCHES, 16, BATCH * GROUP), f32),
            vmem((ROWS, 128), f32),
            vmem((ROWS, 128), f32),
            vmem((ROWS, LATENT), f32),
            vmem((TOK, HEADS * VDIM), bf16),
            vmem((2, PIECES, GROUP, PIECE), bf16),
            vmem((2, PIECES, GROUP, PIECE), bf16),
            vmem((2, PIECES, GROUP, PIECE), f32),
            vmem((2, PIECES, GROUP, PIECE), bf16),
            vmem((2, PIECES, 3, 16, PIECE), bf16),
            vmem((TOK, OUT), bf16),
            dma((6,)),
            dma((2 * SHARDS,)),
            dma((2 * SHARDS,)),
            dma((SHARDS,)),
            dma((SHARDS,)),
            dma((2, PIECES)),
            dma((2, PIECES)),
            dma((2, PIECES, 3)),
            dma((2, PIECES, 3)),
            dma((2, PIECES, 4)),
            dma((2, PIECES, 4)),
            dma((2, PIECES, 3)),
            dma((2, PIECES, 3)),
        ],
        compiler_params=pltpu.CompilerParams(
            collective_id=0, has_side_effects=True, vmem_limit_bytes=56 * 1024 * 1024
        ),
    )(
        group_order,
        q_nope.reshape(TOK, HEADS * NOPE),
        q_rope.reshape(TOK, HEADS * ROPE),
        jnp.transpose(latent_keys, (0, 2, 1)).reshape(LATENT + ROPE, TOK),
        w_uk,
        w_uv,
        o_proj,
    )
    return rows.reshape(1, TOK, OUT)


def solution(mesh):
    placed = (
        P(None, "ctx", "tp"),
        P(None, "ctx", "tp"),
        P(None, "ctx", None),
        P(),
        P("tp", None, None),
        P("tp", None, None),
        P("tp", None),
    )
    return jax.shard_map(
        on_device, mesh=mesh, in_specs=placed, out_specs=P(None, "ctx", None), check_vma=False
    )
```

profile of v0, /device:TPU:1, one launch (start us, length us, event | category | flops | bytes accessed | tf_op | source)
XLA Modules:
  0.0 51.6 jit_solution(3214753127230286328)
XLA Ops:
  0.0 50.7 %shard_map.73 = bf16[128,3584]{1,0:T(8,128)(2,1)S(1)} custom-call(s32[64]{0:T(128)} %order.1, bf16[128,1024]{1,0:T(8,128)(2,1)} %bitcast.7, bf16[128,512]{1,0:T(8,128)(2,1)} %bitcast.9, bf16[576,128]{1,0:T(8,128)(2,1)} %bitcast.8, bf16[8,128,512]{2,1,0:T(8,128)(2,1)} %wuk_hbm.1, bf16[8,512,128]{2,1,0:T(8,128)(2,1)} %wuv_hbm.1, bf16[1024,3584]{1,0:T(8,128)(2,1)} %op_hbm.1), custom_call_target="tpu_custom_call" | custom-call | tf_op jit(solution)/shard_map/pallas_call | solution.py:669
  50.7 0.9 %copy.9 = bf16[1,128,3584]{2,1,0:T(8,128)(2,1)} copy(bf16[1,128,3584]{2,1,0:T(8,128)(2,1)S(1)} %bitcast.6) | data formatting | bytes 1835008
where the time goes:
time: 51.7 us; the launch traced here: 51.6 us
  Pallas kernels  50.7 us (98%)
  local copies, waits for them, and re-layouts  0.93 us (2%)
    pallas_call x1, Pallas kernels, on_device(): pl.pallas_call(attention_kernel, out_shape=pltpu.VMEM((TOK, OUT), bf16),...  50.7 us

commit v1 on v0

--- a/solution.py
+++ b/solution.py
@@ -204,6 +204,7 @@
     ("attend", 6),
     ("attend", 7, (("heads", 0),)),
     ("heads", 1),
+    ("slots",),
     ("exchange", 0),
     ("exchange", 1),
     ("keep", 0),
@@ -212,11 +213,12 @@
     ("keep", 1),
     ("scatter", 0, 1),
     ("scatter", 1, 1),
-    ("settle",),
+    ("settle_gather",),
     ("share", 0, 0),
     ("share", 1, 0),
     ("share", 0, 1),
     ("share", 1, 1),
+    ("settle_output",),
     ("forward", 0, 0),
     ("forward", 1, 0),
     ("forward", 0, 1),
@@ -267,7 +269,6 @@
     own,
     part,
     rsr,
-    obuf,
     load_sem,
     ring_send,
     ring_recv,
@@ -447,7 +448,7 @@
         qa[ROWS // 2 + at : ROWS // 2 + at + GROUP, :LATENT] = absorbed[GROUP:]
         qb[at : at + GROUP, :LATENT] = absorbed[GROUP:]
 
-    def update(rows, scores, values):
+    def soften(rows, scores):
         pieces = [s[:, at : at + 128] for s in scores for at in range(0, s.shape[1], 128)]
         peak = functools.reduce(jnp.maximum, pieces)
         before = top[rows, :]
@@ -456,12 +457,14 @@
         weights = [jnp.exp2(piece - now) for piece in pieces]
         top[rows, :] = now
         total[rows, :] = total[rows, :] * fade + functools.reduce(jnp.add, weights)
+        return fade, [w.astype(jnp.bfloat16) for w in weights]
+
+    def gain(rows, softened, values):
+        fade, weights = softened
         summed = None
         per = len(weights) // len(values)
         for at, value in enumerate(values):
-            mine = jnp.concatenate(
-                [w.astype(jnp.bfloat16) for w in weights[at * per : (at + 1) * per]], 1
-            )
+            mine = jnp.concatenate(weights[at * per : (at + 1) * per], 1)
             part_sum = jnp.dot(mine, value[:, :LATENT], preferred_element_type=jnp.float32)
             summed = part_sum if summed is None else summed + part_sum
         for at in range(0, LATENT, 128):
@@ -490,24 +493,40 @@
 
     low_rows, high_rows = pl.ds(0, ROWS // 2), pl.ds(ROWS // 2, ROWS // 2)
 
-    def score(batch):
+    def attend(batch, between=()):
         for slot in range(batch * BATCH, (batch + 1) * BATCH):
             if slot in pairs:
                 pairs[slot].wait_recv()
         gather_keys(batch)
-        low_low = dot_nt(qa[low_rows, :], klo[...]) + bias[batch, 0:1, :]
-        high_low = dot_nt(qa[high_rows, :], klo[...])
-        high_high = dot_nt(qb[...], khi[...]) + bias[batch, 8:9, :]
-        if batch == 0:
-            low_low, high_high = own_mask(low_low), own_mask(high_high)
-        return [low_low], [high_low, high_high]
-
-    def attend(batch, between=()):
-        low_scores, high_scores = score(batch)
-        update(low_rows, low_scores, [klo])
+
+        def low_low(rows=low_rows):
+            scores = dot_nt(qa[rows, :], klo[...]) + bias[batch, 0:1, :]
+            return own_mask(scores) if batch == 0 else scores
+
+        def high_low(rows=high_rows):
+            return dot_nt(qa[rows, :], klo[...])
+
+        def high_high(rows=pl.ds(0, ROWS // 2)):
+            scores = dot_nt(qb[rows, :], khi[...]) + bias[batch, 8:9, :]
+            return own_mask(scores) if batch == 0 else scores
+
+        n = ROWS // 4
+        a, b = pl.ds(0, n), pl.ds(n, n)
+        ha, hb = pl.ds(2 * n, n), pl.ds(3 * n, n)
+        la = low_low(a)
+        lb = low_low(b)
+        wa = soften(a, [la])
+        hla, hha = high_low(ha), high_high(a)
+        wb = soften(b, [lb])
+        gain(a, wa, [klo])
+        hlb, hhb = high_low(hb), high_high(b)
+        wha = soften(ha, [hla, hha])
+        gain(b, wb, [klo])
         for step in between:
             run(step)
-        update(high_rows, high_scores, [klo, khi])
+        whb = soften(hb, [hlb, hhb])
+        gain(ha, wha, [klo, khi])
+        gain(hb, whb, [klo, khi])
 
     def column(core, piece):
         return pl.multiple_of(core * COLS + piece * PIECE, 128)
@@ -535,7 +554,7 @@
 
     def out_piece(group, piece, chip):
         rows = pl.ds(pl.multiple_of(group * GROUP + chip * 16, 16), 16)
-        return obuf.at[rows, pl.ds(column(c, piece), PIECE)]
+        return out.at[rows, pl.ds(column(c, piece), PIECE)]
 
     def share_copy(group, piece, d):
         block = out_piece(group, piece, x)
@@ -571,6 +590,10 @@
                 context, wuv[head], preferred_element_type=jnp.float32
             ).astype(jnp.bfloat16)
 
+    def to_slots():
+        first, second = sort_rows(flat[...])
+        flat[:GROUP], flat[GROUP:] = first, second
+
     def partial_out(core, piece):
         return jnp.dot(
             flat[...], op[:, pl.ds(column(core, piece), PIECE)], preferred_element_type=jnp.float32
@@ -602,7 +625,7 @@
         for d in range(3):
             summed = summed + rsr[group, piece, d].astype(jnp.float32)
         rows = pl.ds(pl.multiple_of(group * GROUP + x * 16, 16), 16)
-        obuf[rows, pl.ds(column(c, piece), PIECE)] = summed.astype(jnp.bfloat16)
+        out[rows, pl.ds(column(c, piece), PIECE)] = summed.astype(jnp.bfloat16)
         for d in (2, 1, 3, 0):
             share_copy(group, piece, d).start()
 
@@ -610,6 +633,13 @@
         for d in (1, 3, 2):
             share_copy(group, piece, d).wait_recv()
             forward_copy(group, piece, d).start()
+
+    def settle_output():
+        for group in range(2):
+            for piece in range(PIECES):
+                exchange_copy(group, piece).wait_send()
+                for d in (1, 2, 3):
+                    scatter_copy(group, piece, d).wait_send()
 
     def settle_gather():
         for send in SENDS:
@@ -631,7 +661,9 @@
         "scatter": scatter,
         "share": share,
         "forward": forward,
-        "settle": settle_gather,
+        "slots": to_slots,
+        "settle_gather": settle_gather,
+        "settle_output": settle_output,
     }
 
     def run(step):
@@ -648,17 +680,10 @@
         share_copy(group, piece, 0).wait_recv()
         for d in (1, 2, 3):
             forward_copy(group, piece, d).wait_recv()
-    for at in range(0, OUT, PIECE):
-        cols = slice(at, at + PIECE)
-        first, second = sort_rows(obuf[:, cols])
-        out[:GROUP, cols] = first
-        out[GROUP:, cols] = second
     for group, piece in tail:
-        exchange_copy(group, piece).wait_send()
-        share_copy(group, piece, 0).wait_send()
+        for d in (0, 1, 2, 3):
+            share_copy(group, piece, d).wait_send()
         for d in (1, 2, 3):
-            scatter_copy(group, piece, d).wait_send()
-            share_copy(group, piece, d).wait_send()
             forward_copy(group, piece, d).wait_send()
 
 
@@ -694,7 +719,6 @@
             vmem((2, PIECES, GROUP, PIECE), f32),
             vmem((2, PIECES, GROUP, PIECE), bf16),
             vmem((2, PIECES, 3, 16, PIECE), bf16),
-            vmem((TOK, OUT), bf16),
             dma((6,)),
             dma((2 * SHARDS,)),
             dma((2 * SHARDS,)),

time: 51.7 us -> 51 us (0.986)
  Pallas kernels: 50.7 us -> 50 us
    pallas_call x1, Pallas kernels: 50.7 us -> 50 us  [on_device(): pl.pallas_call(attention_kernel, out_shape=pltpu.VMEM((TOK, OUT), bf16),...]
where the time goes in v1:
time: 51 us
  Pallas kernels  50 us (98%)
  local copies, waits for them, and re-layouts  0.93 us (2%)
    pallas_call x1, Pallas kernels, on_device(): pl.pallas_call(attention_kernel, out_shape=pltpu.VMEM((TOK, OUT), bf16),...  50 us

profile of v1, /device:TPU:1, one launch (start us, length us, event | category | flops | bytes accessed | tf_op | source)
XLA Modules:
  0.0 51.0 jit_solution(17980993244978640774)
XLA Ops:
  0.0 50.0 %shard_map.73 = bf16[128,3584]{1,0:T(8,128)(2,1)S(1)} custom-call(s32[64]{0:T(128)} %order.1, bf16[128,1024]{1,0:T(8,128)(2,1)} %bitcast.7, bf16[128,512]{1,0:T(8,128)(2,1)} %bitcast.9, bf16[576,128]{1,0:T(8,128)(2,1)} %bitcast.8, bf16[8,128,512]{2,1,0:T(8,128)(2,1)} %wuk_hbm.1, bf16[8,512,128]{2,1,0:T(8,128)(2,1)} %wuv_hbm.1, bf16[1024,3584]{1,0:T(8,128)(2,1)} %op_hbm.1), custom_call_target="tpu_custom_call" | custom-call | tf_op jit(solution)/shard_map/pallas_call | solution.py:694
  50.0 0.9 %copy.9 = bf16[1,128,3584]{2,1,0:T(8,128)(2,1)} copy(bf16[1,128,3584]{2,1,0:T(8,128)(2,1)S(1)} %bitcast.6) | data formatting | bytes 1835008
